TPU v7x, 512 devices: a whole 4x4x16 slice. The times are simulated.
512 devices in a mesh: fsdp: 16 (over x_lo, y, core), ctx: 32 (over z, x_hi).
Axes of the slice: x: 4 (x_hi: 2, x_lo: 2; x = x_hi * 2 + x_lo), y: 4, z: 16, core: 2. Of those that a mesh axis runs over, the one named last changes fastest.
Arguments:
- tokens: bfloat16 [65536, 8192], P(('fsdp', 'ctx')), may hold values from -2000 to 2000
- doc_of_block: int32 [16, 32], P('fsdp'), may hold values from 0 to 7, never falling along the last dimension, each value on 1 to 17 neighbouring positions
- norm_gain: float32 [8192], replicated, may hold values from 0.1 to 3
- w_query: bfloat16 [8192, 512], P('fsdp'), may hold values from -1 to 1
- w_key: bfloat16 [8192, 128], P('fsdp'), may hold values from -1 to 1
- w_value: bfloat16 [8192, 128], P('fsdp'), may hold values from -0.0625 to 0.0625
Outputs:
- attended: bfloat16 [65536, 512], P(('fsdp', 'ctx'))
Inputs may be any that keep to these rules, and one draw needn't show every extreme that they name: `doc_of_block`: along each row the numbers never fall; each document covers 1 to 17 whole blocks, one exactly 17.
All inputs are finite; a program needn't handle non-finite values.
Results may differ from a plain program's by a relative error of at most 0.0079.
Values may be sent and summed in bfloat16 or wider, within the bound.
A program may use at most 64 MiB of HBM per device.

v0:
```python
import math

import jax
import jax.numpy as jnp
from jax import lax
from jax.sharding import PartitionSpec as P

BLOCK = 128


EPSILON = 1e-05
ROPE_BASE = 500000.0


def shifted(shard, axis, by):
    size = lax.axis_size(axis)
    pairs = [(i, i + by) for i in range(size) if 0 <= i + by < size]
    return lax.ppermute(shard, axis, pairs)


def rotate(inputs, positions):
    half_size = inputs.shape[-1] // 2
    frequencies = ROPE_BASE ** (-2.0 * jnp.arange(half_size, dtype=jnp.float32) / inputs.shape[-1])
    angles = positions.astype(jnp.float32)[:, None] * frequencies[None, :]
    cosine = jnp.cos(angles)[:, None, :]
    sine_part = jnp.sin(angles)[:, None, :]
    first_half = inputs[..., :half_size]
    second_half = inputs[..., half_size:]
    return jnp.concatenate(
        [
            first_half * cosine - second_half * sine_part,
            second_half * cosine + first_half * sine_part,
        ],
        -1,
    )


def normalize(inputs, gain_vector):
    as_float = inputs.astype(jnp.float32)
    mean_square = jnp.mean(as_float * as_float, -1, keepdims=True)
    return (as_float * lax.rsqrt(mean_square + EPSILON) * gain_vector).astype(jnp.bfloat16)


def body(tokens, doc_of_block, norm_gain, w_query, w_key, w_value):
    row_count = tokens.shape[0]
    head_size = w_key.shape[1]
    head_count = w_query.shape[1] // head_size
    normed = normalize(tokens, norm_gain)
    queries = jnp.dot(
        normed,
        lax.all_gather(w_query, "fsdp", axis=0, tiled=True),
        preferred_element_type=jnp.float32,
    )
    keys_local = jnp.dot(
        normed,
        lax.all_gather(w_key, "fsdp", axis=0, tiled=True),
        preferred_element_type=jnp.float32,
    )
    values = jnp.dot(
        normed,
        lax.all_gather(w_value, "fsdp", axis=0, tiled=True),
        preferred_element_type=jnp.float32,
    )
    ctx_rank = lax.axis_index("ctx")
    ctx_count = lax.axis_size("ctx")
    positions = ctx_rank * row_count + jnp.arange(row_count, dtype=jnp.int32)
    queries = rotate(queries.reshape(row_count, head_count, head_size), positions).astype(
        jnp.bfloat16
    )
    queries = queries.transpose(1, 0, 2).reshape(head_count * row_count, head_size)
    keys_local = rotate(keys_local[:, None, :], positions)[:, 0, :].astype(jnp.bfloat16)
    values = values.astype(jnp.bfloat16)
    doc_table = doc_of_block[0]
    block_total = doc_table.shape[0]

    def document_of(token_position):
        matches = (token_position // BLOCK)[:, None] == jnp.arange(block_total, dtype=jnp.int32)[
            None, :
        ]
        return jnp.sum(jnp.where(matches, doc_table[None, :], 0), axis=1)

    query_position = jnp.tile(positions, head_count)
    query_doc = jnp.tile(document_of(positions), head_count)

    def attend(status, key_value, first_row):
        key_position = first_row + jnp.arange(row_count, dtype=jnp.int32)
        allowed = (
            (query_doc[:, None] == document_of(key_position)[None, :])
            & (key_position[None, :] <= query_position[:, None])
            & (key_position[None, :] >= 0)
        )
        running_max, running_sum, running_out = status
        scores = lax.dot_general(
            queries, key_value[0], (((1,), (1,)), ((), ())), preferred_element_type=jnp.float32
        ) / math.sqrt(head_size)
        scores = jnp.where(allowed, scores, -1e30)
        new_max = jnp.maximum(running_max, jnp.max(scores, axis=1))
        decay_factor = jnp.exp(running_max - new_max)
        weights = jnp.where(allowed, jnp.exp(scores - new_max[:, None]), 0.0)
        running_sum = running_sum * decay_factor + jnp.sum(weights, axis=1)
        running_out = running_out * decay_factor[:, None] + jnp.dot(
            weights.astype(jnp.bfloat16), key_value[1], preferred_element_type=jnp.float32
        )
        return (new_max, running_sum, running_out)

    key_value = jnp.stack([keys_local, values])
    status = (
        jnp.full((head_count * row_count,), -1e30, jnp.float32),
        jnp.zeros((head_count * row_count,), jnp.float32),
        jnp.zeros((head_count * row_count, head_size), jnp.float32),
    )

    def chain_step(step_index, carried):
        current, moving = carried
        moving = shifted(moving, "ctx", 1)
        return (attend(current, moving, (ctx_rank - step_index - 1) * row_count), moving)

    status = attend(status, key_value, ctx_rank * row_count)
    status, moving_last = lax.fori_loop(0, ctx_count - 1, chain_step, (status, key_value))
    running_max, running_sum, running_out = status
    result = (running_out / running_sum[:, None]).astype(jnp.bfloat16)
    return (
        result.reshape(head_count, row_count, head_size)
        .transpose(1, 0, 2)
        .reshape(row_count, head_count * head_size)
    )


def solution(mesh):
    placed = (
        P(("fsdp", "ctx"), None),
        P("fsdp", None),
        P(),
        P("fsdp", None),
        P("fsdp", None),
        P("fsdp", None),
    )
    return jax.shard_map(
        body, mesh=mesh, in_specs=placed, out_specs=P(("fsdp", "ctx"), None), check_vma=False
    )
```

profile of v0, /device:TPU:152, one launch (start us, length us, event | category | flops | bytes accessed | tf_op | source)
XLA Modules:
  0.0 502.4 jit_solution(13694992022686083716)
XLA Ops:
  9.6 2.1 fusion.11
  12.0 40.9 %all-gather.6.cloned.1.call-done = bf16[8192,128]{1,0:T(8,128)(2,1)} async-done(((bf16[512,128]{1,0:T(8,128)(2,1)}), bf16[8192,128]{1,0:T(8,128)(2,1)}) %all-gather.6.cloned.1.call-update) | async-done | bytes 2097168 | tf_op jit(solution)/shard_map/all_gather | solution.py:56
  52.9 2.7 convolution_bitcast_fusion
  55.9 40.9 %all-gather.8.cloned.1.call-done = bf16[8192,128]{1,0:T(8,128)(2,1)} async-done(((bf16[512,128]{1,0:T(8,128)(2,1)}), bf16[8192,128]{1,0:T(8,128)(2,1)}) %all-gather.8.cloned.1.call-update) | async-done | bytes 2097168 | tf_op jit(solution)/shard_map/all_gather | solution.py:61
  96.8 2.7 convolution_convert_fusion
  99.7 60.1 %all-gather.4.cloned.1.call-done = bf16[8192,512]{1,0:T(8,128)(2,1)} async-done(((bf16[512,512]{1,0:T(8,128)(2,1)}), bf16[8192,512]{1,0:T(8,128)(2,1)}) %all-gather.4.cloned.1.call-update) | async-done | bytes 8388624 | tf_op jit(solution)/shard_map/all_gather | solution.py:51
  159.8 4.7 fusion.37
  166.0 329.0 %while.23 = (s32[]{:T(128)}, f32[512]{0:T(512)S(1)}, f32[512]{0:T(512)S(1)}, f32[512,128]{1,0:T(8,128)S(1)}, bf16[2,128,128]{2,1,0:T(8,128)(2,1)S(1)}, /*index=5...) while((s32[]{:T(128)}, f32[512]{0:T(512)S(1)}, ...), condition=%wide.region_8.9_spmd.clone, body=%wide.region_4.8_spmd.clone.sunk | while | flops 35077252 | bytes 1957465 | solution.py:119
  166.0 4.6 collective-permute-start
  170.7 5.0 %collective-permute-done = bf16[2,128,128]{2,1,0:T(8,128)(2,1)S(1)} collective-permute-done((bf16[2,128,128]{2,1,0:T(8,128)(2,1)S(1)}, bf16[2,128,128]{2,1,0:T(8,128)(2,1)S(1)}, u32[]{:S(2)}, u32[]{:S(2)}) %collective-permute-start) | collective-permute-done | bytes 65568 | tf_op jit(solution)/shard_map/while/body/eval_jaxpr/ppermute | solution.py:18
  176.5 2.5 collective-permute-start
  179.2 7.2 %collective-permute-done = bf16[2,128,128]{2,1,0:T(8,128)(2,1)S(1)} collective-permute-done((bf16[2,128,128]{2,1,0:T(8,128)(2,1)S(1)}, bf16[2,128,128]{2,1,0:T(8,128)(2,1)S(1)}, u32[]{:S(2)}, u32[]{:S(2)}) %collective-permute-start) | collective-permute-done | bytes 65568 | tf_op jit(solution)/shard_map/while/body/eval_jaxpr/ppermute | solution.py:18
  187.1 1.9 collective-permute-start
  189.2 7.7 %collective-permute-done = bf16[2,128,128]{2,1,0:T(8,128)(2,1)S(1)} collective-permute-done((bf16[2,128,128]{2,1,0:T(8,128)(2,1)S(1)}, bf16[2,128,128]{2,1,0:T(8,128)(2,1)S(1)}, u32[]{:S(2)}, u32[]{:S(2)}) %collective-permute-start) | collective-permute-done | bytes 65568 | tf_op jit(solution)/shard_map/while/body/eval_jaxpr/ppermute | solution.py:18
  197.7 1.9 collective-permute-start
  199.8 7.7 %collective-permute-done = bf16[2,128,128]{2,1,0:T(8,128)(2,1)S(1)} collective-permute-done((bf16[2,128,128]{2,1,0:T(8,128)(2,1)S(1)}, bf16[2,128,128]{2,1,0:T(8,128)(2,1)S(1)}, u32[]{:S(2)}, u32[]{:S(2)}) %collective-permute-start) | collective-permute-done | bytes 65568 | tf_op jit(solution)/shard_map/while/body/eval_jaxpr/ppermute | solution.py:18
  208.3 1.9 collective-permute-start
  210.3 7.7 %collective-permute-done = bf16[2,128,128]{2,1,0:T(8,128)(2,1)S(1)} collective-permute-done((bf16[2,128,128]{2,1,0:T(8,128)(2,1)S(1)}, bf16[2,128,128]{2,1,0:T(8,128)(2,1)S(1)}, u32[]{:S(2)}, u32[]{:S(2)}) %collective-permute-start) | collective-permute-done | bytes 65568 | tf_op jit(solution)/shard_map/while/body/eval_jaxpr/ppermute | solution.py:18
  218.9 1.9 collective-permute-start
  220.9 7.7 %collective-permute-done = bf16[2,128,128]{2,1,0:T(8,128)(2,1)S(1)} collective-permute-done((bf16[2,128,128]{2,1,0:T(8,128)(2,1)S(1)}, bf16[2,128,128]{2,1,0:T(8,128)(2,1)S(1)}, u32[]{:S(2)}, u32[]{:S(2)}) %collective-permute-start) | collective-permute-done | bytes 65568 | tf_op jit(solution)/shard_map/while/body/eval_jaxpr/ppermute | solution.py:18
  229.4 1.9 collective-permute-start
  231.5 7.7 %collective-permute-done = bf16[2,128,128]{2,1,0:T(8,128)(2,1)S(1)} collective-permute-done((bf16[2,128,128]{2,1,0:T(8,128)(2,1)S(1)}, bf16[2,128,128]{2,1,0:T(8,128)(2,1)S(1)}, u32[]{:S(2)}, u32[]{:S(2)}) %collective-permute-start) | collective-permute-done | bytes 65568 | tf_op jit(solution)/shard_map/while/body/eval_jaxpr/ppermute | solution.py:18
  240.0 1.9 collective-permute-start
  242.1 7.8 %collective-permute-done = bf16[2,128,128]{2,1,0:T(8,128)(2,1)S(1)} collective-permute-done((bf16[2,128,128]{2,1,0:T(8,128)(2,1)S(1)}, bf16[2,128,128]{2,1,0:T(8,128)(2,1)S(1)}, u32[]{:S(2)}, u32[]{:S(2)}) %collective-permute-start) | collective-permute-done | bytes 65568 | tf_op jit(solution)/shard_map/while/body/eval_jaxpr/ppermute | solution.py:18
  250.7 1.9 collective-permute-start
  252.7 7.9 %collective-permute-done = bf16[2,128,128]{2,1,0:T(8,128)(2,1)S(1)} collective-permute-done((bf16[2,128,128]{2,1,0:T(8,128)(2,1)S(1)}, bf16[2,128,128]{2,1,0:T(8,128)(2,1)S(1)}, u32[]{:S(2)}, u32[]{:S(2)}) %collective-permute-start) | collective-permute-done | bytes 65568 | tf_op jit(solution)/shard_map/while/body/eval_jaxpr/ppermute | solution.py:18
  261.4 1.9 collective-permute-start
  263.5 7.7 %collective-permute-done = bf16[2,128,128]{2,1,0:T(8,128)(2,1)S(1)} collective-permute-done((bf16[2,128,128]{2,1,0:T(8,128)(2,1)S(1)}, bf16[2,128,128]{2,1,0:T(8,128)(2,1)S(1)}, u32[]{:S(2)}, u32[]{:S(2)}) %collective-permute-start) | collective-permute-done | bytes 65568 | tf_op jit(solution)/shard_map/while/body/eval_jaxpr/ppermute | solution.py:18
  272.0 1.9 collective-permute-start
  274.1 7.7 %collective-permute-done = bf16[2,128,128]{2,1,0:T(8,128)(2,1)S(1)} collective-permute-done((bf16[2,128,128]{2,1,0:T(8,128)(2,1)S(1)}, bf16[2,128,128]{2,1,0:T(8,128)(2,1)S(1)}, u32[]{:S(2)}, u32[]{:S(2)}) %collective-permute-start) | collective-permute-done | bytes 65568 | tf_op jit(solution)/shard_map/while/body/eval_jaxpr/ppermute | solution.py:18
  282.6 1.9 collective-permute-start
  284.6 7.7 %collective-permute-done = bf16[2,128,128]{2,1,0:T(8,128)(2,1)S(1)} collective-permute-done((bf16[2,128,128]{2,1,0:T(8,128)(2,1)S(1)}, bf16[2,128,128]{2,1,0:T(8,128)(2,1)S(1)}, u32[]{:S(2)}, u32[]{:S(2)}) %collective-permute-start) | collective-permute-done | bytes 65568 | tf_op jit(solution)/shard_map/while/body/eval_jaxpr/ppermute | solution.py:18
  293.2 1.9 collective-permute-start
  295.2 7.7 %collective-permute-done = bf16[2,128,128]{2,1,0:T(8,128)(2,1)S(1)} collective-permute-done((bf16[2,128,128]{2,1,0:T(8,128)(2,1)S(1)}, bf16[2,128,128]{2,1,0:T(8,128)(2,1)S(1)}, u32[]{:S(2)}, u32[]{:S(2)}) %collective-permute-start) | collective-permute-done | bytes 65568 | tf_op jit(solution)/shard_map/while/body/eval_jaxpr/ppermute | solution.py:18
  303.7 1.9 collective-permute-start
  305.8 7.7 %collective-permute-done = bf16[2,128,128]{2,1,0:T(8,128)(2,1)S(1)} collective-permute-done((bf16[2,128,128]{2,1,0:T(8,128)(2,1)S(1)}, bf16[2,128,128]{2,1,0:T(8,128)(2,1)S(1)}, u32[]{:S(2)}, u32[]{:S(2)}) %collective-permute-start) | collective-permute-done | bytes 65568 | tf_op jit(solution)/shard_map/while/body/eval_jaxpr/ppermute | solution.py:18
  314.3 1.9 collective-permute-start
  316.4 7.7 %collective-permute-done = bf16[2,128,128]{2,1,0:T(8,128)(2,1)S(1)} collective-permute-done((bf16[2,128,128]{2,1,0:T(8,128)(2,1)S(1)}, bf16[2,128,128]{2,1,0:T(8,128)(2,1)S(1)}, u32[]{:S(2)}, u32[]{:S(2)}) %collective-permute-start) | collective-permute-done | bytes 65568 | tf_op jit(solution)/shard_map/while/body/eval_jaxpr/ppermute | solution.py:18
  324.9 1.9 collective-permute-start
  326.9 7.7 %collective-permute-done = bf16[2,128,128]{2,1,0:T(8,128)(2,1)S(1)} collective-permute-done((bf16[2,128,128]{2,1,0:T(8,128)(2,1)S(1)}, bf16[2,128,128]{2,1,0:T(8,128)(2,1)S(1)}, u32[]{:S(2)}, u32[]{:S(2)}) %collective-permute-start) | collective-permute-done | bytes 65568 | tf_op jit(solution)/shard_map/while/body/eval_jaxpr/ppermute | solution.py:18
  335.5 1.9 collective-permute-start
  337.5 8.3 %collective-permute-done = bf16[2,128,128]{2,1,0:T(8,128)(2,1)S(1)} collective-permute-done((bf16[2,128,128]{2,1,0:T(8,128)(2,1)S(1)}, bf16[2,128,128]{2,1,0:T(8,128)(2,1)S(1)}, u32[]{:S(2)}, u32[]{:S(2)}) %collective-permute-start) | collective-permute-done | bytes 65568 | tf_op jit(solution)/shard_map/while/body/eval_jaxpr/ppermute | solution.py:18
  346.6 1.9 collective-permute-start
  348.7 7.7 %collective-permute-done = bf16[2,128,128]{2,1,0:T(8,128)(2,1)S(1)} collective-permute-done((bf16[2,128,128]{2,1,0:T(8,128)(2,1)S(1)}, bf16[2,128,128]{2,1,0:T(8,128)(2,1)S(1)}, u32[]{:S(2)}, u32[]{:S(2)}) %collective-permute-start) | collective-permute-done | bytes 65568 | tf_op jit(solution)/shard_map/while/body/eval_jaxpr/ppermute | solution.py:18
  357.2 1.9 collective-permute-start
  359.3 7.7 %collective-permute-done = bf16[2,128,128]{2,1,0:T(8,128)(2,1)S(1)} collective-permute-done((bf16[2,128,128]{2,1,0:T(8,128)(2,1)S(1)}, bf16[2,128,128]{2,1,0:T(8,128)(2,1)S(1)}, u32[]{:S(2)}, u32[]{:S(2)}) %collective-permute-start) | collective-permute-done | bytes 65568 | tf_op jit(solution)/shard_map/while/body/eval_jaxpr/ppermute | solution.py:18
  367.8 1.9 collective-permute-start
  369.9 7.7 %collective-permute-done = bf16[2,128,128]{2,1,0:T(8,128)(2,1)S(1)} collective-permute-done((bf16[2,128,128]{2,1,0:T(8,128)(2,1)S(1)}, bf16[2,128,128]{2,1,0:T(8,128)(2,1)S(1)}, u32[]{:S(2)}, u32[]{:S(2)}) %collective-permute-start) | collective-permute-done | bytes 65568 | tf_op jit(solution)/shard_map/while/body/eval_jaxpr/ppermute | solution.py:18
  378.4 1.9 collective-permute-start
  380.4 7.7 %collective-permute-done = bf16[2,128,128]{2,1,0:T(8,128)(2,1)S(1)} collective-permute-done((bf16[2,128,128]{2,1,0:T(8,128)(2,1)S(1)}, bf16[2,128,128]{2,1,0:T(8,128)(2,1)S(1)}, u32[]{:S(2)}, u32[]{:S(2)}) %collective-permute-start) | collective-permute-done | bytes 65568 | tf_op jit(solution)/shard_map/while/body/eval_jaxpr/ppermute | solution.py:18
  389.0 1.9 collective-permute-start
  391.0 7.7 %collective-permute-done = bf16[2,128,128]{2,1,0:T(8,128)(2,1)S(1)} collective-permute-done((bf16[2,128,128]{2,1,0:T(8,128)(2,1)S(1)}, bf16[2,128,128]{2,1,0:T(8,128)(2,1)S(1)}, u32[]{:S(2)}, u32[]{:S(2)}) %collective-permute-start) | collective-permute-done | bytes 65568 | tf_op jit(solution)/shard_map/while/body/eval_jaxpr/ppermute | solution.py:18
  399.5 1.9 collective-permute-start
  401.6 7.7 %collective-permute-done = bf16[2,128,128]{2,1,0:T(8,128)(2,1)S(1)} collective-permute-done((bf16[2,128,128]{2,1,0:T(8,128)(2,1)S(1)}, bf16[2,128,128]{2,1,0:T(8,128)(2,1)S(1)}, u32[]{:S(2)}, u32[]{:S(2)}) %collective-permute-start) | collective-permute-done | bytes 65568 | tf_op jit(solution)/shard_map/while/body/eval_jaxpr/ppermute | solution.py:18
  412.2 7.7 %collective-permute-done = bf16[2,128,128]{2,1,0:T(8,128)(2,1)S(1)} collective-permute-done((bf16[2,128,128]{2,1,0:T(8,128)(2,1)S(1)}, bf16[2,128,128]{2,1,0:T(8,128)(2,1)S(1)}, u32[]{:S(2)}, u32[]{:S(2)}) %collective-permute-start) | collective-permute-done | bytes 65568 | tf_op jit(solution)/shard_map/while/body/eval_jaxpr/ppermute | solution.py:18
  422.7 7.9 %collective-permute-done = bf16[2,128,128]{2,1,0:T(8,128)(2,1)S(1)} collective-permute-done((bf16[2,128,128]{2,1,0:T(8,128)(2,1)S(1)}, bf16[2,128,128]{2,1,0:T(8,128)(2,1)S(1)}, u32[]{:S(2)}, u32[]{:S(2)}) %collective-permute-start) | collective-permute-done | bytes 65568 | tf_op jit(solution)/shard_map/while/body/eval_jaxpr/ppermute | solution.py:18
  433.5 7.8 %collective-permute-done = bf16[2,128,128]{2,1,0:T(8,128)(2,1)S(1)} collective-permute-done((bf16[2,128,128]{2,1,0:T(8,128)(2,1)S(1)}, bf16[2,128,128]{2,1,0:T(8,128)(2,1)S(1)}, u32[]{:S(2)}, u32[]{:S(2)}) %collective-permute-start) | collective-permute-done | bytes 65568 | tf_op jit(solution)/shard_map/while/body/eval_jaxpr/ppermute | solution.py:18
  444.2 7.7 %collective-permute-done = bf16[2,128,128]{2,1,0:T(8,128)(2,1)S(1)} collective-permute-done((bf16[2,128,128]{2,1,0:T(8,128)(2,1)S(1)}, bf16[2,128,128]{2,1,0:T(8,128)(2,1)S(1)}, u32[]{:S(2)}, u32[]{:S(2)}) %collective-permute-start) | collective-permute-done | bytes 65568 | tf_op jit(solution)/shard_map/while/body/eval_jaxpr/ppermute | solution.py:18
  454.7 7.7 %collective-permute-done = bf16[2,128,128]{2,1,0:T(8,128)(2,1)S(1)} collective-permute-done((bf16[2,128,128]{2,1,0:T(8,128)(2,1)S(1)}, bf16[2,128,128]{2,1,0:T(8,128)(2,1)S(1)}, u32[]{:S(2)}, u32[]{:S(2)}) %collective-permute-start) | collective-permute-done | bytes 65568 | tf_op jit(solution)/shard_map/while/body/eval_jaxpr/ppermute | solution.py:18
  465.3 7.7 %collective-permute-done = bf16[2,128,128]{2,1,0:T(8,128)(2,1)S(1)} collective-permute-done((bf16[2,128,128]{2,1,0:T(8,128)(2,1)S(1)}, bf16[2,128,128]{2,1,0:T(8,128)(2,1)S(1)}, u32[]{:S(2)}, u32[]{:S(2)}) %collective-permute-start) | collective-permute-done | bytes 65568 | tf_op jit(solution)/shard_map/while/body/eval_jaxpr/ppermute | solution.py:18
  473.8 1.9 collective-permute-start
  475.9 7.7 %collective-permute-done = bf16[2,128,128]{2,1,0:T(8,128)(2,1)S(1)} collective-permute-done((bf16[2,128,128]{2,1,0:T(8,128)(2,1)S(1)}, bf16[2,128,128]{2,1,0:T(8,128)(2,1)S(1)}, u32[]{:S(2)}, u32[]{:S(2)}) %collective-permute-start) | collective-permute-done | bytes 65568 | tf_op jit(solution)/shard_map/while/body/eval_jaxpr/ppermute | solution.py:18
  484.4 1.9 collective-permute-start
  486.5 7.7 %collective-permute-done = bf16[2,128,128]{2,1,0:T(8,128)(2,1)S(1)} collective-permute-done((bf16[2,128,128]{2,1,0:T(8,128)(2,1)S(1)}, bf16[2,128,128]{2,1,0:T(8,128)(2,1)S(1)}, u32[]{:S(2)}, u32[]{:S(2)}) %collective-permute-start) | collective-permute-done | bytes 65568 | tf_op jit(solution)/shard_map/while/body/eval_jaxpr/ppermute | solution.py:18
  (384 shorter events, 44.1 us)
Async XLA Ops:
  6.5 46.4 %copy-start = (bf16[128,8192]{1,0:T(8,128)(2,1)S(1)}, bf16[128,8192]{1,0:T(8,128)(2,1)}, u32[]{:S(2)}) copy-start(bf16[128,8192]{1,0:T(8,128)(2,1)} %param.8) | copy-start | bytes 6291460
  6.5 46.4 %copy-start.1 = (f32[8192]{0:T(1024)S(1)}, f32[8192]{0:T(1024)}, u32[]{:S(2)}) copy-start(f32[8192]{0:T(1024)} %param.10) | copy-start | bytes 98308
  6.5 46.4 %all-gather.6.cloned.1.call-start = ((), (), s32[]{:S(2)}) async-start(), calls=%async_computation.1 | async-start | bytes 2228224 | tf_op jit(solution)/shard_map/all_gather | solution.py:56
  7.3 89.5 %all-gather.8.cloned.1.call-start = ((), (), s32[]{:S(2)}) async-start(), calls=%async_computation.2 | async-start | bytes 2228224 | tf_op jit(solution)/shard_map/all_gather | solution.py:61
  8.0 151.8 %all-gather.4.cloned.1.call-start = ((), (), s32[]{:S(2)}) async-start(), calls=%async_computation | async-start | bytes 8912896 | tf_op jit(solution)/shard_map/all_gather | solution.py:51
  164.5 1.4 copy-start.2
  166.0 9.8 %collective-permute-start = (bf16[2,128,128]{2,1,0:T(8,128)(2,1)S(1)}, bf16[2,128,128]{2,1,0:T(8,128)(2,1)S(1)}, u32[]{:S(2)}, u32[]{:S(2)}) collective-permute-start(bf16[2,128,128]{2,1,0:T(8,128)(2,1)S(1)} %get-tuple-element.458), channel_id=1, source_target_pairs={{0,1},{1,2},{2,3},{3,4},{4,5},{5,6},{6,7},{7,8},{8,9},{9,10},{10,1... | collective-permute-start | bytes 196616 | tf_op jit(solution)/shard_map/while/body/eval_jaxpr/ppermute | solution.py:18
  176.5 9.8 %collective-permute-start = (bf16[2,128,128]{2,1,0:T(8,128)(2,1)S(1)}, bf16[2,128,128]{2,1,0:T(8,128)(2,1)S(1)}, u32[]{:S(2)}, u32[]{:S(2)}) collective-permute-start(bf16[2,128,128]{2,1,0:T(8,128)(2,1)S(1)} %get-tuple-element.458), channel_id=1, source_target_pairs={{0,1},{1,2},{2,3},{3,4},{4,5},{5,6},{6,7},{7,8},{8,9},{9,10},{10,1... | collective-permute-start | bytes 196616 | tf_op jit(solution)/shard_map/while/body/eval_jaxpr/ppermute | solution.py:18
  187.1 9.8 %collective-permute-start = (bf16[2,128,128]{2,1,0:T(8,128)(2,1)S(1)}, bf16[2,128,128]{2,1,0:T(8,128)(2,1)S(1)}, u32[]{:S(2)}, u32[]{:S(2)}) collective-permute-start(bf16[2,128,128]{2,1,0:T(8,128)(2,1)S(1)} %get-tuple-element.458), channel_id=1, source_target_pairs={{0,1},{1,2},{2,3},{3,4},{4,5},{5,6},{6,7},{7,8},{8,9},{9,10},{10,1... | collective-permute-start | bytes 196616 | tf_op jit(solution)/shard_map/while/body/eval_jaxpr/ppermute | solution.py:18
  197.7 9.8 %collective-permute-start = (bf16[2,128,128]{2,1,0:T(8,128)(2,1)S(1)}, bf16[2,128,128]{2,1,0:T(8,128)(2,1)S(1)}, u32[]{:S(2)}, u32[]{:S(2)}) collective-permute-start(bf16[2,128,128]{2,1,0:T(8,128)(2,1)S(1)} %get-tuple-element.458), channel_id=1, source_target_pairs={{0,1},{1,2},{2,3},{3,4},{4,5},{5,6},{6,7},{7,8},{8,9},{9,10},{10,1... | collective-permute-start | bytes 196616 | tf_op jit(solution)/shard_map/while/body/eval_jaxpr/ppermute | solution.py:18
  208.3 9.8 %collective-permute-start = (bf16[2,128,128]{2,1,0:T(8,128)(2,1)S(1)}, bf16[2,128,128]{2,1,0:T(8,128)(2,1)S(1)}, u32[]{:S(2)}, u32[]{:S(2)}) collective-permute-start(bf16[2,128,128]{2,1,0:T(8,128)(2,1)S(1)} %get-tuple-element.458), channel_id=1, source_target_pairs={{0,1},{1,2},{2,3},{3,4},{4,5},{5,6},{6,7},{7,8},{8,9},{9,10},{10,1... | collective-permute-start | bytes 196616 | tf_op jit(solution)/shard_map/while/body/eval_jaxpr/ppermute | solution.py:18
  218.9 9.8 %collective-permute-start = (bf16[2,128,128]{2,1,0:T(8,128)(2,1)S(1)}, bf16[2,128,128]{2,1,0:T(8,128)(2,1)S(1)}, u32[]{:S(2)}, u32[]{:S(2)}) collective-permute-start(bf16[2,128,128]{2,1,0:T(8,128)(2,1)S(1)} %get-tuple-element.458), channel_id=1, source_target_pairs={{0,1},{1,2},{2,3},{3,4},{4,5},{5,6},{6,7},{7,8},{8,9},{9,10},{10,1... | collective-permute-start | bytes 196616 | tf_op jit(solution)/shard_map/while/body/eval_jaxpr/ppermute | solution.py:18
  229.4 9.8 %collective-permute-start = (bf16[2,128,128]{2,1,0:T(8,128)(2,1)S(1)}, bf16[2,128,128]{2,1,0:T(8,128)(2,1)S(1)}, u32[]{:S(2)}, u32[]{:S(2)}) collective-permute-start(bf16[2,128,128]{2,1,0:T(8,128)(2,1)S(1)} %get-tuple-element.458), channel_id=1, source_target_pairs={{0,1},{1,2},{2,3},{3,4},{4,5},{5,6},{6,7},{7,8},{8,9},{9,10},{10,1... | collective-permute-start | bytes 196616 | tf_op jit(solution)/shard_map/while/body/eval_jaxpr/ppermute | solution.py:18
  240.0 9.8 %collective-permute-start = (bf16[2,128,128]{2,1,0:T(8,128)(2,1)S(1)}, bf16[2,128,128]{2,1,0:T(8,128)(2,1)S(1)}, u32[]{:S(2)}, u32[]{:S(2)}) collective-permute-start(bf16[2,128,128]{2,1,0:T(8,128)(2,1)S(1)} %get-tuple-element.458), channel_id=1, source_target_pairs={{0,1},{1,2},{2,3},{3,4},{4,5},{5,6},{6,7},{7,8},{8,9},{9,10},{10,1... | collective-permute-start | bytes 196616 | tf_op jit(solution)/shard_map/while/body/eval_jaxpr/ppermute | solution.py:18
  250.7 10.0 %collective-permute-start = (bf16[2,128,128]{2,1,0:T(8,128)(2,1)S(1)}, bf16[2,128,128]{2,1,0:T(8,128)(2,1)S(1)}, u32[]{:S(2)}, u32[]{:S(2)}) collective-permute-start(bf16[2,128,128]{2,1,0:T(8,128)(2,1)S(1)} %get-tuple-element.458), channel_id=1, source_target_pairs={{0,1},{1,2},{2,3},{3,4},{4,5},{5,6},{6,7},{7,8},{8,9},{9,10},{10,1... | collective-permute-start | bytes 196616 | tf_op jit(solution)/shard_map/while/body/eval_jaxpr/ppermute | solution.py:18
  261.4 9.8 %collective-permute-start = (bf16[2,128,128]{2,1,0:T(8,128)(2,1)S(1)}, bf16[2,128,128]{2,1,0:T(8,128)(2,1)S(1)}, u32[]{:S(2)}, u32[]{:S(2)}) collective-permute-start(bf16[2,128,128]{2,1,0:T(8,128)(2,1)S(1)} %get-tuple-element.458), channel_id=1, source_target_pairs={{0,1},{1,2},{2,3},{3,4},{4,5},{5,6},{6,7},{7,8},{8,9},{9,10},{10,1... | collective-permute-start | bytes 196616 | tf_op jit(solution)/shard_map/while/body/eval_jaxpr/ppermute | solution.py:18
  272.0 9.8 %collective-permute-start = (bf16[2,128,128]{2,1,0:T(8,128)(2,1)S(1)}, bf16[2,128,128]{2,1,0:T(8,128)(2,1)S(1)}, u32[]{:S(2)}, u32[]{:S(2)}) collective-permute-start(bf16[2,128,128]{2,1,0:T(8,128)(2,1)S(1)} %get-tuple-element.458), channel_id=1, source_target_pairs={{0,1},{1,2},{2,3},{3,4},{4,5},{5,6},{6,7},{7,8},{8,9},{9,10},{10,1... | collective-permute-start | bytes 196616 | tf_op jit(solution)/shard_map/while/body/eval_jaxpr/ppermute | solution.py:18
  282.6 9.8 %collective-permute-start = (bf16[2,128,128]{2,1,0:T(8,128)(2,1)S(1)}, bf16[2,128,128]{2,1,0:T(8,128)(2,1)S(1)}, u32[]{:S(2)}, u32[]{:S(2)}) collective-permute-start(bf16[2,128,128]{2,1,0:T(8,128)(2,1)S(1)} %get-tuple-element.458), channel_id=1, source_target_pairs={{0,1},{1,2},{2,3},{3,4},{4,5},{5,6},{6,7},{7,8},{8,9},{9,10},{10,1... | collective-permute-start | bytes 196616 | tf_op jit(solution)/shard_map/while/body/eval_jaxpr/ppermute | solution.py:18
  293.2 9.8 %collective-permute-start = (bf16[2,128,128]{2,1,0:T(8,128)(2,1)S(1)}, bf16[2,128,128]{2,1,0:T(8,128)(2,1)S(1)}, u32[]{:S(2)}, u32[]{:S(2)}) collective-permute-start(bf16[2,128,128]{2,1,0:T(8,128)(2,1)S(1)} %get-tuple-element.458), channel_id=1, source_target_pairs={{0,1},{1,2},{2,3},{3,4},{4,5},{5,6},{6,7},{7,8},{8,9},{9,10},{10,1... | collective-permute-start | bytes 196616 | tf_op jit(solution)/shard_map/while/body/eval_jaxpr/ppermute | solution.py:18
  303.7 9.8 %collective-permute-start = (bf16[2,128,128]{2,1,0:T(8,128)(2,1)S(1)}, bf16[2,128,128]{2,1,0:T(8,128)(2,1)S(1)}, u32[]{:S(2)}, u32[]{:S(2)}) collective-permute-start(bf16[2,128,128]{2,1,0:T(8,128)(2,1)S(1)} %get-tuple-element.458), channel_id=1, source_target_pairs={{0,1},{1,2},{2,3},{3,4},{4,5},{5,6},{6,7},{7,8},{8,9},{9,10},{10,1... | collective-permute-start | bytes 196616 | tf_op jit(solution)/shard_map/while/body/eval_jaxpr/ppermute | solution.py:18
  314.3 9.8 %collective-permute-start = (bf16[2,128,128]{2,1,0:T(8,128)(2,1)S(1)}, bf16[2,128,128]{2,1,0:T(8,128)(2,1)S(1)}, u32[]{:S(2)}, u32[]{:S(2)}) collective-permute-start(bf16[2,128,128]{2,1,0:T(8,128)(2,1)S(1)} %get-tuple-element.458), channel_id=1, source_target_pairs={{0,1},{1,2},{2,3},{3,4},{4,5},{5,6},{6,7},{7,8},{8,9},{9,10},{10,1... | collective-permute-start | bytes 196616 | tf_op jit(solution)/shard_map/while/body/eval_jaxpr/ppermute | solution.py:18
  324.9 9.8 %collective-permute-start = (bf16[2,128,128]{2,1,0:T(8,128)(2,1)S(1)}, bf16[2,128,128]{2,1,0:T(8,128)(2,1)S(1)}, u32[]{:S(2)}, u32[]{:S(2)}) collective-permute-start(bf16[2,128,128]{2,1,0:T(8,128)(2,1)S(1)} %get-tuple-element.458), channel_id=1, source_target_pairs={{0,1},{1,2},{2,3},{3,4},{4,5},{5,6},{6,7},{7,8},{8,9},{9,10},{10,1... | collective-permute-start | bytes 196616 | tf_op jit(solution)/shard_map/while/body/eval_jaxpr/ppermute | solution.py:18
  335.5 10.4 %collective-permute-start = (bf16[2,128,128]{2,1,0:T(8,128)(2,1)S(1)}, bf16[2,128,128]{2,1,0:T(8,128)(2,1)S(1)}, u32[]{:S(2)}, u32[]{:S(2)}) collective-permute-start(bf16[2,128,128]{2,1,0:T(8,128)(2,1)S(1)} %get-tuple-element.458), channel_id=1, source_target_pairs={{0,1},{1,2},{2,3},{3,4},{4,5},{5,6},{6,7},{7,8},{8,9},{9,10},{10,1... | collective-permute-start | bytes 196616 | tf_op jit(solution)/shard_map/while/body/eval_jaxpr/ppermute | solution.py:18
  346.6 9.8 %collective-permute-start = (bf16[2,128,128]{2,1,0:T(8,128)(2,1)S(1)}, bf16[2,128,128]{2,1,0:T(8,128)(2,1)S(1)}, u32[]{:S(2)}, u32[]{:S(2)}) collective-permute-start(bf16[2,128,128]{2,1,0:T(8,128)(2,1)S(1)} %get-tuple-element.458), channel_id=1, source_target_pairs={{0,1},{1,2},{2,3},{3,4},{4,5},{5,6},{6,7},{7,8},{8,9},{9,10},{10,1... | collective-permute-start | bytes 196616 | tf_op jit(solution)/shard_map/while/body/eval_jaxpr/ppermute | solution.py:18
  357.2 9.8 %collective-permute-start = (bf16[2,128,128]{2,1,0:T(8,128)(2,1)S(1)}, bf16[2,128,128]{2,1,0:T(8,128)(2,1)S(1)}, u32[]{:S(2)}, u32[]{:S(2)}) collective-permute-start(bf16[2,128,128]{2,1,0:T(8,128)(2,1)S(1)} %get-tuple-element.458), channel_id=1, source_target_pairs={{0,1},{1,2},{2,3},{3,4},{4,5},{5,6},{6,7},{7,8},{8,9},{9,10},{10,1... | collective-permute-start | bytes 196616 | tf_op jit(solution)/shard_map/while/body/eval_jaxpr/ppermute | solution.py:18
  367.8 9.8 %collective-permute-start = (bf16[2,128,128]{2,1,0:T(8,128)(2,1)S(1)}, bf16[2,128,128]{2,1,0:T(8,128)(2,1)S(1)}, u32[]{:S(2)}, u32[]{:S(2)}) collective-permute-start(bf16[2,128,128]{2,1,0:T(8,128)(2,1)S(1)} %get-tuple-element.458), channel_id=1, source_target_pairs={{0,1},{1,2},{2,3},{3,4},{4,5},{5,6},{6,7},{7,8},{8,9},{9,10},{10,1... | collective-permute-start | bytes 196616 | tf_op jit(solution)/shard_map/while/body/eval_jaxpr/ppermute | solution.py:18
  378.4 9.8 %collective-permute-start = (bf16[2,128,128]{2,1,0:T(8,128)(2,1)S(1)}, bf16[2,128,128]{2,1,0:T(8,128)(2,1)S(1)}, u32[]{:S(2)}, u32[]{:S(2)}) collective-permute-start(bf16[2,128,128]{2,1,0:T(8,128)(2,1)S(1)} %get-tuple-element.458), channel_id=1, source_target_pairs={{0,1},{1,2},{2,3},{3,4},{4,5},{5,6},{6,7},{7,8},{8,9},{9,10},{10,1... | collective-permute-start | bytes 196616 | tf_op jit(solution)/shard_map/while/body/eval_jaxpr/ppermute | solution.py:18
  389.0 9.8 %collective-permute-start = (bf16[2,128,128]{2,1,0:T(8,128)(2,1)S(1)}, bf16[2,128,128]{2,1,0:T(8,128)(2,1)S(1)}, u32[]{:S(2)}, u32[]{:S(2)}) collective-permute-start(bf16[2,128,128]{2,1,0:T(8,128)(2,1)S(1)} %get-tuple-element.458), channel_id=1, source_target_pairs={{0,1},{1,2},{2,3},{3,4},{4,5},{5,6},{6,7},{7,8},{8,9},{9,10},{10,1... | collective-permute-start | bytes 196616 | tf_op jit(solution)/shard_map/while/body/eval_jaxpr/ppermute | solution.py:18
  399.5 9.8 %collective-permute-start = (bf16[2,128,128]{2,1,0:T(8,128)(2,1)S(1)}, bf16[2,128,128]{2,1,0:T(8,128)(2,1)S(1)}, u32[]{:S(2)}, u32[]{:S(2)}) collective-permute-start(bf16[2,128,128]{2,1,0:T(8,128)(2,1)S(1)} %get-tuple-element.458), channel_id=1, source_target_pairs={{0,1},{1,2},{2,3},{3,4},{4,5},{5,6},{6,7},{7,8},{8,9},{9,10},{10,1... | collective-permute-start | bytes 196616 | tf_op jit(solution)/shard_map/while/body/eval_jaxpr/ppermute | solution.py:18
  410.1 9.8 %collective-permute-start = (bf16[2,128,128]{2,1,0:T(8,128)(2,1)S(1)}, bf16[2,128,128]{2,1,0:T(8,128)(2,1)S(1)}, u32[]{:S(2)}, u32[]{:S(2)}) collective-permute-start(bf16[2,128,128]{2,1,0:T(8,128)(2,1)S(1)} %get-tuple-element.458), channel_id=1, source_target_pairs={{0,1},{1,2},{2,3},{3,4},{4,5},{5,6},{6,7},{7,8},{8,9},{9,10},{10,1... | collective-permute-start | bytes 196616 | tf_op jit(solution)/shard_map/while/body/eval_jaxpr/ppermute | solution.py:18
  420.7 10.0 %collective-permute-start = (bf16[2,128,128]{2,1,0:T(8,128)(2,1)S(1)}, bf16[2,128,128]{2,1,0:T(8,128)(2,1)S(1)}, u32[]{:S(2)}, u32[]{:S(2)}) collective-permute-start(bf16[2,128,128]{2,1,0:T(8,128)(2,1)S(1)} %get-tuple-element.458), channel_id=1, source_target_pairs={{0,1},{1,2},{2,3},{3,4},{4,5},{5,6},{6,7},{7,8},{8,9},{9,10},{10,1... | collective-permute-start | bytes 196616 | tf_op jit(solution)/shard_map/while/body/eval_jaxpr/ppermute | solution.py:18
  431.5 9.8 %collective-permute-start = (bf16[2,128,128]{2,1,0:T(8,128)(2,1)S(1)}, bf16[2,128,128]{2,1,0:T(8,128)(2,1)S(1)}, u32[]{:S(2)}, u32[]{:S(2)}) collective-permute-start(bf16[2,128,128]{2,1,0:T(8,128)(2,1)S(1)} %get-tuple-element.458), channel_id=1, source_target_pairs={{0,1},{1,2},{2,3},{3,4},{4,5},{5,6},{6,7},{7,8},{8,9},{9,10},{10,1... | collective-permute-start | bytes 196616 | tf_op jit(solution)/shard_map/while/body/eval_jaxpr/ppermute | solution.py:18
  442.1 9.8 %collective-permute-start = (bf16[2,128,128]{2,1,0:T(8,128)(2,1)S(1)}, bf16[2,128,128]{2,1,0:T(8,128)(2,1)S(1)}, u32[]{:S(2)}, u32[]{:S(2)}) collective-permute-start(bf16[2,128,128]{2,1,0:T(8,128)(2,1)S(1)} %get-tuple-element.458), channel_id=1, source_target_pairs={{0,1},{1,2},{2,3},{3,4},{4,5},{5,6},{6,7},{7,8},{8,9},{9,10},{10,1... | collective-permute-start | bytes 196616 | tf_op jit(solution)/shard_map/while/body/eval_jaxpr/ppermute | solution.py:18
  452.7 9.8 %collective-permute-start = (bf16[2,128,128]{2,1,0:T(8,128)(2,1)S(1)}, bf16[2,128,128]{2,1,0:T(8,128)(2,1)S(1)}, u32[]{:S(2)}, u32[]{:S(2)}) collective-permute-start(bf16[2,128,128]{2,1,0:T(8,128)(2,1)S(1)} %get-tuple-element.458), channel_id=1, source_target_pairs={{0,1},{1,2},{2,3},{3,4},{4,5},{5,6},{6,7},{7,8},{8,9},{9,10},{10,1... | collective-permute-start | bytes 196616 | tf_op jit(solution)/shard_map/while/body/eval_jaxpr/ppermute | solution.py:18
  463.2 9.8 %collective-permute-start = (bf16[2,128,128]{2,1,0:T(8,128)(2,1)S(1)}, bf16[2,128,128]{2,1,0:T(8,128)(2,1)S(1)}, u32[]{:S(2)}, u32[]{:S(2)}) collective-permute-start(bf16[2,128,128]{2,1,0:T(8,128)(2,1)S(1)} %get-tuple-element.458), channel_id=1, source_target_pairs={{0,1},{1,2},{2,3},{3,4},{4,5},{5,6},{6,7},{7,8},{8,9},{9,10},{10,1... | collective-permute-start | bytes 196616 | tf_op jit(solution)/shard_map/while/body/eval_jaxpr/ppermute | solution.py:18
  473.8 9.8 %collective-permute-start = (bf16[2,128,128]{2,1,0:T(8,128)(2,1)S(1)}, bf16[2,128,128]{2,1,0:T(8,128)(2,1)S(1)}, u32[]{:S(2)}, u32[]{:S(2)}) collective-permute-start(bf16[2,128,128]{2,1,0:T(8,128)(2,1)S(1)} %get-tuple-element.458), channel_id=1, source_target_pairs={{0,1},{1,2},{2,3},{3,4},{4,5},{5,6},{6,7},{7,8},{8,9},{9,10},{10,1... | collective-permute-start | bytes 196616 | tf_op jit(solution)/shard_map/while/body/eval_jaxpr/ppermute | solution.py:18
  484.4 9.8 %collective-permute-start = (bf16[2,128,128]{2,1,0:T(8,128)(2,1)S(1)}, bf16[2,128,128]{2,1,0:T(8,128)(2,1)S(1)}, u32[]{:S(2)}, u32[]{:S(2)}) collective-permute-start(bf16[2,128,128]{2,1,0:T(8,128)(2,1)S(1)} %get-tuple-element.458), channel_id=1, source_target_pairs={{0,1},{1,2},{2,3},{3,4},{4,5},{5,6},{6,7},{7,8},{8,9},{9,10},{10,1... | collective-permute-start | bytes 196616 | tf_op jit(solution)/shard_map/while/body/eval_jaxpr/ppermute | solution.py:18
Sparse Core Ops, SparseCore 0:
  9.5 43.3 all-gather.5
  55.1 41.7 all-gather.7
  99.0 60.8 all-gather.3
where the time goes:
time: 504 us; the launch traced here: 502 us
  waiting for transfers between devices  381 us (76%)
  starting transfers between devices  62.8 us (12%)
  matrix products  28.5 us (6%)
  between operations  13.3 us (3%)
  other arithmetic  12.8 us (3%)
    ppermute x31, waiting for transfers between devices, shifted(): return lax.ppermute(shard, axis, pairs)  237 us
    ppermute x31, starting transfers between devices, shifted(): return lax.ppermute(shard, axis, pairs)  62.8 us
    all_gather x1, waiting for transfers between devices, body(): lax.all_gather(w_query, 'fsdp', axis=0, tiled=True)  60.1 us
    all_gather x1, waiting for transfers between devices, body(): lax.all_gather(w_key, 'fsdp', axis=0, tiled=True)  40.9 us
    all_gather x1, waiting for transfers between devices, body(): lax.all_gather(w_value, 'fsdp', axis=0, tiled=True)  40.9 us
    dot_general x32, matrix products, attend(): jnp.dot(weights.astype(jnp.bfloat16), key_value[1], preferred_element_typ...  11.5 us
  transfers between devices with their start and end apart: 34, of which 34 were waited for; matrix products, arithmetic and copies ran while one was open for 2% of the time, Pallas kernels for 0%

commit v1 on v0

v1 whole, which is shorter than its diff:
```python
import functools
import math

import jax
import jax.numpy as jnp
import numpy as np
from jax import lax
from jax.experimental import pallas as pl
from jax.experimental.pallas import tpu as pltpu
from jax.sharding import PartitionSpec as P

BLOCK = 128
EPSILON = 1e-05
ROPE_BASE = 500000.0
NEG = -1e30
MESH = pl.DeviceIdType.MESH

EDGES = ((0, 3), (0, 1), (3, 6), (3, 4), (3, 2), (6, 8), (6, 7), (6, 5))
REACH = 8
GROUPS = ((0, 4), (4, 7), (7, 9))


def tables(blocks, head):
    half = head // 2
    freq = (ROPE_BASE ** (-2.0 * np.arange(half, dtype=np.float64) / head)).astype(np.float32).astype(np.float64)
    freq = np.concatenate([freq, freq])[None, :]
    inner = np.arange(BLOCK, dtype=np.float64)[:, None] * freq
    outer = np.arange(blocks, dtype=np.float64)[:, None] * BLOCK * freq
    return [t.astype(np.float32) for t in (np.cos(inner), np.sin(inner), np.cos(outer), np.sin(outer))]


def kernel(
    tok, gain, wq_in, wk_in, wv_in, cos_in, sin_in, cos_out, sin_out, doc, out,
    xbuf, tbuf, wkv, wq, kvb, pf_kv, pr_kv, pf_q, pr_q, qs,
    tok_s, tok_r, wy_s, wy_r, wc_s, wc_r, pp_s, pp_r, z_s, z_r, xp_s, xp_r,
):
    f = lax.axis_index("fsdp")
    ctx = lax.axis_index("ctx")
    xl, y, c = f // 8, (f // 2) % 4, f % 2
    z, xh = ctx // 2, ctx % 2
    x = xh * 2 + xl

    def at_x(nx):
        nx = nx % 4
        return {"fsdp": (nx % 2) * 8 + y * 2 + c, "ctx": z * 2 + nx // 2}

    def at_y(ny):
        return {"fsdp": xl * 8 + (ny % 4) * 2 + c, "ctx": ctx}

    def at_z(nz):
        return {"fsdp": f, "ctx": (nz % 16) * 2 + xh}

    sib = {"fsdp": xl * 8 + y * 2 + (1 - c), "ctx": ctx}
    ahead, behind = at_x(x + 5 - 2 * c), at_x(x + 3 + 2 * c)
    partner = at_x(x + 2)
    ys = (y + 1, y + 3, y + 2)

    barrier = pltpu.get_barrier_semaphore()
    friends = [ahead, behind, partner, sib] + [at_y(v) for v in ys]
    friends += [at_z(z + d) for d in (1, 15, 2, 14, 3, 13)]
    for who in friends:
        pl.semaphore_signal(barrier, inc=1, device_id=who, device_id_type=MESH)

    def remote(src, dst, send, recv, who):
        return pltpu.make_async_remote_copy(
            src_ref=src, dst_ref=dst, send_sem=send, recv_sem=recv, device_id=who, device_id_type=MESH
        )

    mine = y * 2 + c
    def add_square(j, acc):
        v = tok[:, pl.ds(pl.multiple_of(j * 512, 512), 512)].astype(jnp.float32)
        v = v * v
        return acc + (v[:, :128] + v[:, 128:256]) + (v[:, 256:384] + v[:, 384:])

    total = lax.fori_loop(0, 16, add_square, jnp.zeros((BLOCK, 128), jnp.float32))
    scale = lax.rsqrt(jnp.sum(total, axis=1, keepdims=True) / 8192.0 + EPSILON)

    def norm_slot(s, carry):
        for other in (1, 0):
            group = xl if other == 0 else 1 - xl
            cols = pl.ds(pl.multiple_of(group * 4096 + s * 512, 512), 512)
            v = (tok[:, cols].astype(jnp.float32) * scale * gain[:, cols]).astype(jnp.bfloat16)
            if other:
                tbuf[s] = v
            else:
                xbuf[s, 0:128, :] = v
        return carry

    lax.fori_loop(0, 8, norm_slot, 0)
    wkv[mine, :, 0:128] = wk_in[...]
    wkv[mine, :, 128:256] = wv_in[...]
    wq[mine] = wq_in[...]

    pl.semaphore_wait(barrier, len(friends))

    toks = [
        remote(tbuf.at[s], xbuf.at[s, pl.ds(128, 128)], tok_s.at[s], tok_r.at[s], ahead) for s in range(8)
    ]
    wkv_y = [remote(wkv.at[mine], wkv.at[mine], wy_s.at[i], wy_r.at[i], at_y(ys[i])) for i in range(3)]
    wq_y = [remote(wq.at[mine], wq.at[mine], wy_s.at[3 + i], wy_r.at[3 + i], at_y(ys[i])) for i in range(3)]
    froms = [((y + 3) % 4) * 2 + c, ((y + 1) % 4) * 2 + c, ((y + 2) % 4) * 2 + c]
    wkv_in = [remote(wkv.at[s], wkv.at[s], wy_s.at[i], wy_r.at[i], at_y(ys[i])) for i, s in enumerate(froms)]
    wq_got = [remote(wq.at[s], wq.at[s], wy_s.at[3 + i], wy_r.at[3 + i], at_y(ys[i])) for i, s in enumerate(froms)]
    held = [mine] + froms

    def to_sibling(buf, base, i):
        return remote(buf.at[held[i]], buf.at[held[i]], wc_s.at[base + i], wc_r.at[base + i], sib)

    def from_sibling(buf, base, i):
        s = held[i] + 1 - 2 * c
        return remote(buf.at[s], buf.at[s], wc_s.at[base + i], wc_r.at[base + i], sib)

    for i in range(3):
        wkv_y[i].start()
    for t in toks:
        t.start()
    to_sibling(wkv, 0, 0).start()
    to_sibling(wq, 4, 0).start()
    for i in range(3):
        wkv_y[i].wait_send()
    for i in range(3):
        wq_y[i].start()
    for i in range(3):
        wkv_in[i].wait_recv()
        to_sibling(wkv, 0, 1 + i).start()
    for i in range(4):
        from_sibling(wkv, 0, i).wait_recv()
    for t in toks:
        t.wait_recv()

    def project(buf, width):
        def step(s, acc):
            return acc + jnp.dot(xbuf[s], buf[s], preferred_element_type=jnp.float32)

        return lax.fori_loop(0, 8, step, jnp.zeros((256, width), jnp.float32))

    acc = project(wkv, 256)
    pf_kv[...] = acc[128:]
    back_kv = remote(pf_kv, pr_kv, pp_s.at[0], pp_r.at[0], behind)
    back_kv.start()
    co, so = cos_out[pl.ds(ctx, 1), :], sin_out[pl.ds(ctx, 1), :]
    cosine = co * cos_in[...] - so * sin_in[...]
    sine = so * cos_in[...] + co * sin_in[...]
    lane = lax.broadcasted_iota(jnp.int32, (BLOCK, 128), 1)
    sine = jnp.where(lane < 64, -sine, sine)

    def rotate(v):
        return (v * cosine + pltpu.roll(v, 64, 1) * sine).astype(jnp.bfloat16)

    back_kv.wait_recv()
    own = acc[:128] + pr_kv[...]
    kvb[0, 0, :, 0:128] = rotate(own[:, :128])
    kvb[0, 0, :, 128:256] = own[:, 128:].astype(jnp.bfloat16)

    edges = {
        (a, b): remote(kvb.at[0, a], kvb.at[0, b], z_s.at[b - 1], z_r.at[b - 1], at_z(z + b - a + 16))
        for a, b in EDGES
    }
    across = [remote(kvb.at[0, d], kvb.at[1, d], xp_s.at[d], xp_r.at[d], partner) for d in range(REACH + 1)]

    def pass_on(d):
        if d:
            edges[next(e for e in EDGES if e[1] == d)].wait_recv()
        for a, b in EDGES:
            if a == d:
                edges[(a, b)].start()
        across[d].start()

    for d in (0, 3, 1, 6, 2, 4):
        pass_on(d)
    for i in range(3):
        wq_got[i].wait_recv()
        to_sibling(wq, 4, 1 + i).start()
    for i in range(4):
        from_sibling(wq, 4, i).wait_recv()
    acc_q = project(wq, 512)
    pf_q[...] = acc_q[128:]
    back_q = remote(pf_q, pr_q, pp_s.at[1], pp_r.at[1], behind)
    back_q.start()
    for d in (5, 7, 8):
        pass_on(d)
    back_q.wait_recv()
    for h in range(4):
        cols = slice(h * 128, (h + 1) * 128)
        qs[cols, :] = rotate(acc_q[:128, cols] + pr_q[:, cols])

    my_doc = doc[0, ctx]

    def bias_of(block):
        ok = (block >= 0) & (block <= ctx) & (doc[0, jnp.clip(block, 0, 31)] == my_doc)
        return jnp.where(ok, 0.0, NEG).astype(jnp.float32)

    row = lax.broadcasted_iota(jnp.int32, (512, 128), 0) % BLOCK
    col = lax.broadcasted_iota(jnp.int32, (512, 128), 1)
    triangle = jnp.where(col <= row, 0.0, NEG)
    state = None
    for first, last in GROUPS:
        n = last - first
        for d in range(first, last):
            across[d].wait_recv()
        keys = kvb[:, first:last, :, 0:128].reshape(2 * n * BLOCK, 128)
        vals = kvb[:, first:last, :, 128:256].reshape(2 * n * BLOCK, 128)
        scores = lax.dot_general(qs[...], keys, (((1,), (1,)), ((), ())), preferred_element_type=jnp.float32)
        bias = jnp.concatenate(
            [
                jnp.full((1, BLOCK), bias_of(ctx - 2 * d + lane_at * (1 - 2 * xh)), jnp.float32)
                for lane_at in (0, 1)
                for d in range(first, last)
            ],
            axis=1,
        )
        scores = scores * (1.0 / math.sqrt(128.0)) + bias
        if first == 0:
            scores = jnp.concatenate([scores[:, :128] + triangle, scores[:, 128:]], axis=1)
        top = jnp.max(scores, axis=1, keepdims=True)
        if state is not None:
            top = jnp.maximum(state[0], top)
        weights = jnp.exp(scores - top)
        sums = jnp.sum(weights, axis=1, keepdims=True)
        outs = jnp.dot(weights.astype(jnp.bfloat16), vals, preferred_element_type=jnp.float32)
        if state is not None:
            decay = jnp.exp(state[0] - top)
            sums, outs = sums + state[1] * decay, outs + state[2] * decay
        state = (top, sums, outs)
    result = (state[2] / state[1]).astype(jnp.bfloat16)
    for h in range(4):
        out[:, h * 128 : (h + 1) * 128] = result[h * 128 : (h + 1) * 128, :]

    for copy in toks + wq_y + [back_kv, back_q] + across + [edges[e] for e in EDGES]:
        copy.wait_send()
    for i in range(4):
        to_sibling(wkv, 0, i).wait_send()
        to_sibling(wq, 4, i).wait_send()


def body(tokens, doc_of_block, norm_gain, w_query, w_key, w_value):
    vmem, smem = pl.BlockSpec(memory_space=pltpu.VMEM), pl.BlockSpec(memory_space=pltpu.SMEM)
    dma = pltpu.SemaphoreType.DMA
    bf, fl = jnp.bfloat16, jnp.float32
    return pl.pallas_call(
        kernel,
        out_shape=jax.ShapeDtypeStruct((128, 512), bf),
        in_specs=[vmem] * 9 + [smem],
        out_specs=vmem,
        scratch_shapes=[
            pltpu.VMEM((8, 256, 512), bf),
            pltpu.VMEM((8, 128, 512), bf),
            pltpu.VMEM((8, 512, 256), bf),
            pltpu.VMEM((8, 512, 512), bf),
            pltpu.VMEM((2, REACH + 1, 128, 256), bf),
            pltpu.VMEM((128, 256), fl),
            pltpu.VMEM((128, 256), fl),
            pltpu.VMEM((128, 512), fl),
            pltpu.VMEM((128, 512), fl),
            pltpu.VMEM((512, 128), bf),
            dma((8,)), dma((8,)),
            dma((6,)), dma((6,)),
            dma((8,)), dma((8,)),
            dma((2,)), dma((2,)),
            dma((REACH,)), dma((REACH,)),
            dma((REACH + 1,)), dma((REACH + 1,)),
        ],
        compiler_params=pltpu.CompilerParams(
            collective_id=0, has_side_effects=True, vmem_limit_bytes=48 * 2**20
        ),
    )(
        tokens, norm_gain.reshape(1, -1), w_query, w_key, w_value,
        *[jnp.asarray(t) for t in tables(32, 128)], doc_of_block,
    )


def solution(mesh):
    placed = (
        P(("fsdp", "ctx"), None),
        P("fsdp", None),
        P(),
        P("fsdp", None),
        P("fsdp", None),
        P("fsdp", None),
    )
    return jax.shard_map(
        body, mesh=mesh, in_specs=placed, out_specs=P(("fsdp", "ctx"), None), check_vma=False
    )
```

time: 504 us -> 79.3 us (0.16)
  the two profiles are of different devices: /device:TPU:152 before, /device:TPU:9 now
where the time goes in v1:
time: 79.3 us; the launch traced here: 78.8 us
  Pallas kernels  69.2 us (87%)
  local copies, waits for them, and re-layouts  9.62 us (12%)
    pallas_call x1, Pallas kernels, body(): pl.pallas_call(kernel, out_shape=jax.ShapeDtypeStruct((128, 512), bf), in...  69.2 us
    unnamed x21, local copies, waits for them, and re-layouts  9.62 us

profile of v1, /device:TPU:9, one launch (start us, length us, event | category | flops | bytes accessed | tf_op | source)
XLA Modules:
  0.0 78.8 jit_solution(4378494618269161438)
XLA Ops:
  0.0 0.0 copy-start
  0.0 1.6 %copy-done = bf16[128,8192]{1,0:T(8,128)(2,1)S(1)} copy-done((bf16[128,8192]{1,0:T(8,128)(2,1)S(1)}, bf16[128,8192]{1,0:T(8,128)(2,1)}, u32[]{:S(2)}) %copy-start) | copy-done | bytes 2097176
  1.6 0.0 copy-start.1
  1.6 1.0 %copy-done.1 = bf16[512,512]{1,0:T(8,128)(2,1)S(1)} copy-done((bf16[512,512]{1,0:T(8,128)(2,1)S(1)}, bf16[512,512]{1,0:T(8,128)(2,1)}, u32[]{:S(2)}) %copy-start.1) | copy-done | bytes 524312
  2.6 0.0 copy-start.2
  2.6 0.9 %copy-done.2 = bf16[512,128]{1,0:T(8,128)(2,1)S(1)} copy-done((bf16[512,128]{1,0:T(8,128)(2,1)S(1)}, bf16[512,128]{1,0:T(8,128)(2,1)}, u32[]{:S(2)}) %copy-start.2) | copy-done | bytes 131096
  3.5 0.0 copy-start.3
  3.5 0.9 %copy-done.3 = bf16[512,128]{1,0:T(8,128)(2,1)S(1)} copy-done((bf16[512,128]{1,0:T(8,128)(2,1)S(1)}, bf16[512,128]{1,0:T(8,128)(2,1)}, u32[]{:S(2)}) %copy-start.3) | copy-done | bytes 131096
  4.4 0.0 copy-start.4
  4.4 0.8 %copy-done.4 = f32[128,128]{1,0:T(8,128)S(1)} copy-done((f32[128,128]{1,0:T(8,128)S(1)}, f32[128,128]{1,0:T(8,128)}, u32[]{:S(2)}) %copy-start.4) | copy-done | bytes 65560
  5.3 0.0 copy-start.5
  5.3 0.8 %copy-done.5 = f32[128,128]{1,0:T(8,128)S(1)} copy-done((f32[128,128]{1,0:T(8,128)S(1)}, f32[128,128]{1,0:T(8,128)}, u32[]{:S(2)}) %copy-start.5) | copy-done | bytes 65560
  6.1 0.0 copy-start.6
  6.1 0.8 copy-done.6
  6.9 0.0 copy-start.7
  6.9 0.7 copy-done.7
  7.6 0.0 copy-start.8
  7.6 0.7 copy-done.8
  8.3 0.0 copy-start.9
  8.3 0.7 copy-done.9
  9.0 69.2 %shard_map.100 = bf16[128,512]{1,0:T(8,128)(2,1)S(1)} custom-call(bf16[128,8192]{1,0:T(8,128)(2,1)S(1)} %copy-done, f32[1,8192]{1,0:T(1,128)S(1)} %bitcast.1, bf16[512,512]{1,0:T(8,128)(2,1)S(1)} %copy-done.1, bf16[512,128]{1,0:T(8,128)(2,1)S(1)} %copy-done.2, bf16[512,128]{1,0:T(8,128)(2,1)S(1)} %copy-done.3, f32[128,128]{1,0:T(8,128)S(1)} %copy-done.5, ...), custom_call_target="tpu_custom_call" | custom-call | tf_op jit(solution)/shard_map/pallas_call | solution.py:240
  78.2 0.7 copy.12
Async XLA Ops:
  0.0 1.6 %copy-start = (bf16[128,8192]{1,0:T(8,128)(2,1)S(1)}, bf16[128,8192]{1,0:T(8,128)(2,1)}, u32[]{:S(2)}) copy-start(bf16[128,8192]{1,0:T(8,128)(2,1)} %tok.1) | copy-start | bytes 6291460
  1.6 1.0 %copy-start.1 = (bf16[512,512]{1,0:T(8,128)(2,1)S(1)}, bf16[512,512]{1,0:T(8,128)(2,1)}, u32[]{:S(2)}) copy-start(bf16[512,512]{1,0:T(8,128)(2,1)} %wq_in.1) | copy-start | bytes 1572868
  2.6 0.9 %copy-start.2 = (bf16[512,128]{1,0:T(8,128)(2,1)S(1)}, bf16[512,128]{1,0:T(8,128)(2,1)}, u32[]{:S(2)}) copy-start(bf16[512,128]{1,0:T(8,128)(2,1)} %wk_in.1) | copy-start | bytes 393220
  3.5 0.9 %copy-start.3 = (bf16[512,128]{1,0:T(8,128)(2,1)S(1)}, bf16[512,128]{1,0:T(8,128)(2,1)}, u32[]{:S(2)}) copy-start(bf16[512,128]{1,0:T(8,128)(2,1)} %wv_in.1) | copy-start | bytes 393220
  4.4 0.8 %copy-start.4 = (f32[128,128]{1,0:T(8,128)S(1)}, f32[128,128]{1,0:T(8,128)}, u32[]{:S(2)}) copy-start(f32[128,128]{1,0:T(8,128)} %constant.9.clone.sin_in) | copy-start | bytes 196612
  5.3 0.8 %copy-start.5 = (f32[128,128]{1,0:T(8,128)S(1)}, f32[128,128]{1,0:T(8,128)}, u32[]{:S(2)}) copy-start(f32[128,128]{1,0:T(8,128)} %constant.8.clone.cos_in) | copy-start | bytes 196612
  6.1 0.8 copy-start.6
  6.9 0.7 copy-start.7
  7.6 0.7 copy-start.8
  8.3 0.7 copy-start.9
